TPU v7x, 512 devices: a whole 4x4x16 slice. The times are simulated.
512 devices in a mesh: grp: 32 (over y, x, core), mem: 16 (over z).
Axes of the slice: x: 4, y: 4, z: 16, core: 2. Of those that a mesh axis runs over, the one named last changes fastest.
Arguments:
- tensor_blocks: bfloat16 [4096, 256, 256], P(('grp', 'mem')), may hold values from -6 to 6
- block_coords: int32 [4, 4096], P(None, ('grp', 'mem')), may hold values from 0 to 127, as said below
- live_count: int32 [32, 16], P('grp', 'mem'), may hold values from 6 to 8, as said below
- owner_order: int32 [16, 128], P('mem'), may hold values from 0 to 127, as said below
- factor_two: bfloat16 [16384, 256], P(('grp', 'mem'))
- factor_three: bfloat16 [16384, 256], P(('grp', 'mem'))
- factor_four: bfloat16 [16384, 256], P(('grp', 'mem'))
Outputs:
- new_factor: float32 [16, 2048, 256], P('mem', 'grp')
Inputs may be any that keep to these rules, and one draw needn't show every extreme that they name: `block_coords`: rows 1 to 3 lie in 0 to 31. Among one device's live slots, the row-0 entries that fall in one owner's positions (owner g owns positions g * 4 to (g + 1) * 4 - 1 of owner_order[m]) take at most 2 distinct values, and on every device exactly 2 for some owner. `live_count`: some device is full in every draw. `owner_order`: each row is a permutation of 0 to 127.
All inputs are finite; a program needn't handle non-finite values.
Results may differ from a plain program's by a relative error of at most 0.0035.
Values may be sent and summed in bfloat16 or wider, within the bound.
A program may use at most 64 MiB of HBM per device.

v0:
```python
import jax
import jax.numpy as jnp
from jax import lax
from jax.sharding import PartitionSpec as P

B = 16


def gram_matrix(factor):
    return lax.dot_general(
        factor, factor, (((0,), (0,)), ((), ())), preferred_element_type=jnp.float32
    )


def cholesky_lower(system):
    size = system.shape[0]
    index = jnp.arange(size, dtype=jnp.int32)

    def column(step, lower):
        row_now = lax.dynamic_index_in_dim(lower, step, 0, keepdims=False)
        target = lax.dynamic_index_in_dim(system, step, 1, keepdims=False)
        corner = lax.dynamic_index_in_dim(target, step, 0, keepdims=False)
        pivot = jnp.sqrt(corner - jnp.dot(row_now, row_now, precision=lax.Precision.HIGHEST))
        values = (target - jnp.dot(lower, row_now, precision=lax.Precision.HIGHEST)) / pivot
        values = jnp.where(
            index > step, values, jnp.where(index == step, pivot, jnp.zeros_like(values))
        )
        return lax.dynamic_update_index_in_dim(lower, values[:, None], step, 1)

    return lax.fori_loop(jnp.int32(0), jnp.int32(size), column, jnp.zeros_like(system))


def solve_rows(system, sums):
    lower = cholesky_lower(system)
    size = system.shape[0]

    def forward(step, solved):
        row_now = lax.dynamic_index_in_dim(lower, step, 0, keepdims=False)
        pivot = lax.dynamic_index_in_dim(row_now, step, 0, keepdims=False)
        given = lax.dynamic_index_in_dim(sums, step, 1, keepdims=False)
        values = (given - jnp.dot(solved, row_now, precision=lax.Precision.HIGHEST)) / pivot
        return lax.dynamic_update_index_in_dim(solved, values[:, None], step, 1)

    middle = lax.fori_loop(jnp.int32(0), jnp.int32(size), forward, jnp.zeros_like(sums))

    def backward(count, solved):
        step = (size - 1 - count).astype(jnp.int32)
        col_now = lax.dynamic_index_in_dim(lower, step, 1, keepdims=False)
        pivot = lax.dynamic_index_in_dim(col_now, step, 0, keepdims=False)
        given = lax.dynamic_index_in_dim(middle, step, 1, keepdims=False)
        values = (given - jnp.dot(solved, col_now, precision=lax.Precision.HIGHEST)) / pivot
        return lax.dynamic_update_index_in_dim(solved, values[:, None], step, 1)

    return lax.fori_loop(jnp.int32(0), jnp.int32(size), backward, jnp.zeros_like(sums))


def on_device(
    tensor_blocks, block_coords, live_count, owner_order, factor_two, factor_three, factor_four
):
    block_total = tensor_blocks.shape[0]
    factor_rank = factor_two.shape[1]
    block_edge = B
    groups = lax.axis_size("grp")
    slab_rows = owner_order.shape[1]
    owned_blocks = slab_rows // groups
    whole_two, whole_three, whole_four = (
        lax.all_gather(factor_two, "mem", axis=0, tiled=True),
        lax.all_gather(factor_three, "mem", axis=0, tiled=True),
        lax.all_gather(factor_four, "mem", axis=0, tiled=True),
    )
    table_two = whole_two.reshape(-1, block_edge, factor_rank)
    table_three = whole_three.reshape(-1, block_edge, factor_rank)
    table_four = whole_four.reshape(-1, block_edge, factor_rank)
    owner_ids = owner_order[0]
    slab_index = jnp.arange(slab_rows, dtype=jnp.int32)
    positions = jnp.sum(
        jnp.where(owner_ids[None, :] == block_coords[0][:, None], slab_index[None, :], 0), axis=1
    )
    live_total = live_count[0, 0]
    live_mask = jnp.arange(block_total, dtype=jnp.int32) < live_total

    def add_batch(batch, totals):
        first_block = batch * 4
        values_batch = lax.dynamic_slice_in_dim(tensor_blocks, first_block, 4, 0)
        coords_batch = lax.dynamic_slice_in_dim(block_coords, first_block, 4, 1)
        where_batch = lax.dynamic_slice_in_dim(positions, first_block, 4, 0)
        mask_batch = lax.dynamic_slice_in_dim(live_mask, first_block, 4, 0)
        first_rows = jnp.take(table_two, coords_batch[1], axis=0)
        second_rows = jnp.take(table_three, coords_batch[2], axis=0)
        third_rows = jnp.take(table_four, coords_batch[3], axis=0)
        khatri = (
            (
                second_rows[:, :, None, :].astype(jnp.float32)
                * third_rows[:, None, :, :].astype(jnp.float32)
            )
            .reshape(4, block_edge * block_edge, factor_rank)
            .astype(jnp.bfloat16)
        )
        product = jnp.einsum(
            "bij,bjr->bir", values_batch, khatri, preferred_element_type=jnp.float32
        )
        partial_value = jnp.sum(
            product.reshape(4, block_edge, block_edge, factor_rank)
            * first_rows[:, None, :, :].astype(jnp.float32),
            axis=2,
        )
        selector = ((slab_index[:, None] == where_batch[None, :]) & mask_batch[None, :]).astype(
            jnp.float32
        )
        return totals + jnp.dot(
            selector, partial_value.reshape(4, -1), precision=lax.Precision.HIGHEST
        )

    totals = lax.fori_loop(
        jnp.int32(0),
        (live_total + 3) // 4,
        add_batch,
        jnp.zeros((slab_rows, block_edge * factor_rank), jnp.float32),
    )
    gram_parts = lax.psum(
        (gram_matrix(factor_two), gram_matrix(factor_three), gram_matrix(factor_four)),
        ("grp", "mem"),
    )
    system = gram_parts[0] * gram_parts[1] * gram_parts[2]
    owned_sum = lax.psum_scatter(totals, "grp", scatter_dimension=0, tiled=True)
    solved = solve_rows(system, owned_sum.reshape(owned_blocks * block_edge, factor_rank))
    return solved.reshape(1, owned_blocks * block_edge, factor_rank)


def solution(mesh):
    return jax.shard_map(
        on_device,
        mesh=mesh,
        in_specs=(
            P(("grp", "mem"), None, None),
            P(None, ("grp", "mem")),
            P("grp", "mem"),
            P("mem", None),
            P(("grp", "mem"), None),
            P(("grp", "mem"), None),
            P(("grp", "mem"), None),
        ),
        out_specs=P("mem", "grp", None),
        check_vma=False,
    )
```

profile of v0, /device:TPU:1, one launch (start us, length us, event | category | flops | bytes accessed | tf_op | source)
XLA Modules:
  0.0 2198.5 jit_solution(14834301434695923107)
XLA Ops:
  6.5 1.7 fusion.24
  8.3 1.7 fusion.25
  10.0 1.8 fusion.26
  12.5 33.4 %all_gather.9 = bf16[512,256]{1,0:T(8,128)(2,1)} all-gather(bf16[32,256]{1,0:T(8,128)(2,1)} %param.22), channel_id=1, replica_groups=mesh['grp'=32,'mem'=16] {'mem'}, dimensions={0}, use_global_device_ids=true | all-gather | bytes 278528 | tf_op jit(solution)/shard_map/all_gather | solution.py:68
  45.8 23.2 %all_gather.10 = bf16[512,256]{1,0:T(8,128)(2,1)} all-gather(bf16[32,256]{1,0:T(8,128)(2,1)} %param.23), channel_id=1, replica_groups=mesh['grp'=32,'mem'=16] {'mem'}, dimensions={0}, use_global_device_ids=true | all-gather | bytes 278528 | tf_op jit(solution)/shard_map/all_gather | solution.py:69
  69.0 25.7 %all_gather.11 = bf16[512,256]{1,0:T(8,128)(2,1)} all-gather(bf16[32,256]{1,0:T(8,128)(2,1)S(1)} %copy-done.2), channel_id=1, replica_groups=mesh['grp'=32,'mem'=16] {'mem'}, dimensions={0}, use_global_device_ids=true | all-gather | bytes 278528 | tf_op jit(solution)/shard_map/all_gather | solution.py:67
  95.2 13.9 while.54
  95.3 1.5 gather_fusion.1
  96.8 1.5 gather_fusion
  98.4 1.5 gather_fusion.2
  100.7 1.4 convolution_add_fusion.2
  102.2 1.5 gather_fusion.1
  103.8 1.5 gather_fusion
  105.4 1.5 gather_fusion.2
  107.7 1.4 convolution_add_fusion.2
  109.1 1.3 copy-done
  110.4 1.3 dynamic-slice.15
  112.2 375.3 %all-reduce.7.cloned.1.call-done = (f32[256,256]{1,0:T(8,128)}, f32[256,256]{1,0:T(8,128)}, f32[256,256]{1,0:T(8,128)}) async-done(((f32[256,256]{1,0:T(8,128)}, f32[256,256]{1,0:T(8,128)}, f32[256,256]{1,0:T(8,128)}), (f32[256,256]{1,0:T(8,128)}, f32[256,256]{1,0:T(8,128)}, f32[256,256]{1,0:T(8,128)})) %all-reduce.7.cloned.1.call-update) | async-done | bytes 786448 | tf_op jit(solution)/shard_map/psum | solution.py:120
  487.5 1.2 multiply_multiply_fusion
  488.8 960.3 %while.55 = (s32[]{:T(128)}, f32[256,256]{1,0:T(8,128)S(1)}, f32[256,256]{0,1:T(8,128)S(1)}, s32[]{:T(128)}, s32[]{:T(128)}, /*index=5*/s32[]{:T(128)}) while((s32[]{:T(128)}, f32[256,256]{1,0:T(8,128)S(1)}, f32[256,256]{0,1:T(8,128)S(1)}, s32[]{:T(128)}, s32[]{:T(128)}, /*index=5*/s32[]{:T(128)}) %tuple.127), condition=%wide.region_4.5_spmd.clone.clone, body=%wide.region_3.4_spmd.clone.clone.sunk | while | flops 788483 | bytes 276621 | solution.py:30
  1449.3 0.9 constant_dynamic-slice_fusion.3
  1450.4 369.3 %while.52 = (s32[]{:T(128)}, f32[64,256]{0,1:T(8,128)S(1)}, f32[64,256]{0,1:T(8,128)S(1)}, f32[256,256]{1,0:T(8,128)S(1)}, s32[]{:T(128)}, /*index=5*/s32[]{:T(128)}, s32[]{:T(128)}) while((s32[]{:T(128)}, f32[64,256]{0,1:T(8,128)S(1)}, f32[64,256]{0,1:T(8,128)S(1)}, f32[256,256]{1,0:T(8,128)S(1)}, s32[]{:T(128)}, /*index=5*/s32[]{:T(128)}, ...), condition=%wide.region_11.13_spmd, body=%wide.region_10.12_spmd.sunk | while | flops 196739 | bytes 135021 | solution.py:44
  1452.5 0.8 fusion.52
  1455.3 0.8 fusion.52
  1458.2 0.8 fusion.52
  1462.5 0.8 fusion.52
  1465.4 0.8 fusion.52
  1468.3 0.8 fusion.52
  1469.8 0.8 fusion.52
  1472.6 0.8 fusion.52
  1475.5 0.8 fusion.52
  1479.9 0.8 fusion.52
  1482.7 0.8 fusion.52
  1485.6 0.8 fusion.52
  1490.0 0.8 fusion.52
  1492.8 0.8 fusion.52
  1495.7 0.8 fusion.52
  1497.2 0.8 fusion.52
  1500.1 0.8 fusion.52
  1502.9 0.8 fusion.52
  1507.3 0.8 fusion.52
  1510.2 0.8 fusion.52
  1513.0 0.8 fusion.52
  1517.4 0.8 fusion.52
  1520.3 0.8 fusion.52
  1523.1 0.8 fusion.52
  1524.6 0.8 fusion.52
  1819.7 371.2 %while.53 = (s32[]{:T(128)}, f32[64,256]{0,1:T(8,128)S(1)}, f32[64,256]{0,1:T(8,128)S(1)}, f32[256,256]{0,1:T(8,128)S(1)}, s32[]{:T(128)}, /*index=5*/s32[]{:T(128)}, s32[]{:T(128)}, s32[]{:T(128)}) while((s32[]{:T(128)}, f32[64,256]{0,1:T(8,128)S(1)}, f32[64,256]{0,1:T(8,128)S(1)}, f32[256,256]{0,1:T(8,128)S(1)}, s32[]{:T(128)}, ...), condition=%wide.region_13.15_spmd, body=%wide.region_12.14_spmd.sunk | while | flops 196743 | bytes 134567 | solution.py:54
  (3609 shorter events, 1317.8 us)
Async XLA Ops:
  6.5 62.5 %copy-start.2 = (bf16[32,256]{1,0:T(8,128)(2,1)S(1)}, bf16[32,256]{1,0:T(8,128)(2,1)}, u32[]{:S(2)}) copy-start(bf16[32,256]{1,0:T(8,128)(2,1)} %param.21) | copy-start | bytes 49156
  6.5 88.2 %copy-start.3 = (s32[4,8]{1,0:T(4,128)S(1)}, s32[4,8]{1,0:T(4,128)}, u32[]{:S(2)}) copy-start(s32[4,8]{1,0:T(4,128)} %param.18) | copy-start | bytes 388
  6.5 88.2 %copy-start.4 = (s32[1,128]{1,0:T(1,128)S(1)}, s32[1,128]{1,0:T(1,128)}, u32[]{:S(2)}) copy-start(s32[1,128]{1,0:T(1,128)} %param.20) | copy-start | bytes 1540
  6.5 481.0 %all-reduce.7.cloned.1.call-start = ((), (), s32[]{:S(2)}) async-start(), calls=%async_computation.1 | async-start | bytes 1572864 | tf_op jit(solution)/shard_map/psum | solution.py:120
  10.0 85.2 %copy-start.1 = (bf16[8,256,256]{2,1,0:T(8,128)(2,1)S(1)}, bf16[8,256,256]{2,1,0:T(8,128)(2,1)}, u32[]{:S(2)}) copy-start(bf16[8,256,256]{2,1,0:T(8,128)(2,1)} %param.17) | copy-start | bytes 3145732
  11.8 1437.5 %all-reduce.5.cloned.1.call-start = ((), (), s32[]{:S(2)}) async-start(), calls=%async_computation | async-start | bytes 4194304
  109.1 1.3 copy-start
Sparse Core Ops, SparseCore 0:
  13.1 474.3 all-reduce.6
  491.1 137.5 all-reduce.4
where the time goes:
time: 2240 us; the launch traced here: 2200 us
  local copies, waits for them, and re-layouts  716 us (32%)
  matrix products  478 us (21%)
  waiting for transfers between devices  375 us (17%)
  loops' own time  367 us (16%)
  other arithmetic  165 us (7%)
  blocking collectives  82.3 us (4%)
    psum x1, waiting for transfers between devices, on_device(): lax.psum((gram_matrix(factor_two), gram_matrix(factor_three), gram_matrix...  375 us
    another operation x1, loops' own time, cholesky_lower(): lax.fori_loop(jnp.int32(0), jnp.int32(size), column, jnp.zeros_like(system))  355 us
    dot_general x256, matrix products, backward(): jnp.dot(solved, col_now, precision=lax.Precision.HIGHEST)  201 us
    dot_general x256, matrix products, forward(): jnp.dot(solved, row_now, precision=lax.Precision.HIGHEST)  201 us
    dynamic_slice x256, local copies, waits for them, and re-layouts, column(): corner = lax.dynamic_index_in_dim(target, step, 0, keepdims=False)  166 us
    dot_general x256, other arithmetic, column(): jnp.dot(row_now, row_now, precision=lax.Precision.HIGHEST)  161 us
    dynamic_update_slice x256, local copies, waits for them, and re-layouts, column(): return lax.dynamic_update_index_in_dim(lower, values[:, None], step, 1)  157 us
    dynamic_slice x256, local copies, waits for them, and re-layouts, forward(): pivot = lax.dynamic_index_in_dim(row_now, step, 0, keepdims=False)  153 us
  transfers between devices with their start and end apart: 2, of which 1 were waited for; matrix products, arithmetic and copies ran while one was open for 28% of the time, Pallas kernels for 0%

commit v1 on v0

v1 whole, which is shorter than its diff:
```python
import functools

import jax
import jax.numpy as jnp
from jax import lax
from jax.experimental import pallas as pl
from jax.experimental.pallas import tpu as pltpu
from jax.sharding import PartitionSpec as P

B = 16
R = 256
HALF = 128
OWNED = 4
NONE = 9999
MESH = pl.DeviceIdType.MESH


def dot_full(a, b, along_a=1, along_b=0):
    return lax.dot_general(
        a,
        b,
        (((along_a,), (along_b,)), ((), ())),
        precision=lax.Precision.HIGHEST,
        preferred_element_type=jnp.float32,
    )


def invert_half(ref):
    panels = HALF // 8
    lane = lax.broadcasted_iota(jnp.int32, (8, HALF), 1)
    row = lax.broadcasted_iota(jnp.int32, (8, HALF), 0)
    for panel in range(panels):
        first = panel * 8
        whole = ref[...]
        columns = [
            jnp.broadcast_to(whole[:, first + j : first + j + 1], (HALF, HALF)) for j in range(8)
        ]
        corner = [column[first : first + 8] for column in columns]
        inside = (lane >= first) & (lane < first + 8)
        pivots = jnp.where(
            inside, jnp.where(lane - first == row, 1.0, 0.0), whole[first : first + 8]
        )
        for j in range(8):
            inverse = 1.0 / jnp.broadcast_to(corner[j][j : j + 1], (8, HALF))
            scaled = jnp.broadcast_to(pivots[j : j + 1], (8, HALF)) * inverse
            here = row == j
            pivots = jnp.where(here, scaled, pivots - corner[j] * scaled)
            for k in range(j + 1, 8):
                factor = jnp.broadcast_to(corner[k][j : j + 1], (8, HALF)) * inverse
                corner[k] = jnp.where(here, factor, corner[k] - corner[j] * factor)
        for i in range(panels):
            at = i * 8
            if i == panel:
                ref[at : at + 8, :] = pivots
            else:
                part = jnp.where(inside, 0.0, whole[at : at + 8])
                for j in range(8):
                    part = part - columns[j][at : at + 8] * jnp.broadcast_to(
                        pivots[j : j + 1], (8, HALF)
                    )
                ref[at : at + 8, :] = part


def solve_kernel(system_ref, sums_ref, out_ref, first_ref, second_ref):
    first_ref[...] = system_ref[0:HALF, 0:HALF]
    invert_half(first_ref)
    first = first_ref[...]
    cross = system_ref[0:HALF, HALF:R]
    weights = dot_full(first, cross)
    second_ref[...] = system_ref[HALF:R, HALF:R] - dot_full(cross, weights, 0, 0)
    left = sums_ref[:, 0:HALF]
    invert_half(second_ref)
    right = dot_full(sums_ref[:, HALF:R] - dot_full(left, weights), second_ref[...])
    out_ref[:, HALF:R] = right
    out_ref[:, 0:HALF] = dot_full(left, first) - dot_full(right, weights, 1, 1)


def solve_rows(system, sums):
    return pl.pallas_call(
        solve_kernel,
        out_shape=jax.ShapeDtypeStruct(sums.shape, jnp.float32),
        scratch_shapes=[pltpu.VMEM((HALF, HALF), jnp.float32)] * 2,
        name="solve_rows",
    )(system, sums)


def gather_kernel(
    groups,
    members,
    coords_ref,
    live_ref,
    order_ref,
    blocks_ref,
    two_ref,
    three_ref,
    four_ref,
    system_ref,
    sums_ref,
    blocks,
    table,
    parts,
    gram_out,
    gram_in,
    system,
    rows_out,
    rows_in,
    code_out,
    code_in,
    lows,
    highs,
    block_sem,
    ring_send,
    ring_recv,
    gram_send,
    gram_recv,
    system_send,
    system_recv,
    rows_send,
    rows_recv,
    code_send,
    code_recv,
):
    group = lax.axis_index("grp")
    member = lax.axis_index("mem")
    slots = blocks.shape[0]
    owned = two_ref.shape[0] // B
    half_way = members // 2
    after = lax.rem(member + 1, members)
    before = lax.rem(member + members - 1, members)

    load = pltpu.make_async_copy(blocks_ref, blocks, block_sem)
    load.start()

    barrier = pltpu.get_barrier_semaphore()
    for neighbour in (after, before):
        pl.semaphore_signal(barrier, inc=1, device_id={"mem": neighbour}, device_id_type=MESH)

    def greet(step, carry):
        pl.semaphore_signal(
            barrier,
            inc=1,
            device_id={"grp": lax.rem(group + step, groups)},
            device_id_type=MESH,
        )
        return carry

    lax.fori_loop(1, groups, greet, 0)
    for mode, ref in enumerate((two_ref, three_ref, four_ref)):
        for i in range(owned):
            table[mode, member * owned + i] = ref[i * B : (i + 1) * B, :]
    pl.semaphore_wait(barrier, groups + 1)

    def hop(way, step, mode, source):
        chunk = table.at[mode, pl.ds(source * owned, owned)]
        return pltpu.make_async_remote_copy(
            src_ref=chunk,
            dst_ref=chunk,
            send_sem=ring_send.at[way, step, mode],
            recv_sem=ring_recv.at[way, step, mode],
            device_id={"mem": after if way == 0 else before},
            device_id_type=MESH,
        )

    def sent(way, step):
        shift = step if way == 1 else members - step
        return lax.rem(member + shift, members)

    def arrived(way, step):
        shift = step + 1 if way == 1 else members - step - 1
        return lax.rem(member + shift, members)

    def last_way(mode):
        return 0 if mode < 2 else 1

    for mode in range(3):
        for way in range(2):
            hop(way, 0, mode, sent(way, 0)).start()

    live = live_ref[0, 0]
    wanted = [coords_ref[0, j] for j in range(slots)]

    def find(place, found):
        here = order_ref[0, place]
        return tuple(jnp.where(here == c, place, f) for c, f in zip(wanted, found))

    found = lax.fori_loop(0, groups * OWNED, find, (jnp.int32(0),) * slots, unroll=4)
    places = [jnp.where(j < live, found[j], -NONE) for j in range(slots)]
    code_row = lax.broadcasted_iota(jnp.int32, (8, R), 0)

    def send_to(buffer_out, buffer_in, send_sem, recv_sem, target):
        return pltpu.make_async_remote_copy(
            src_ref=buffer_out.at[target],
            dst_ref=buffer_in.at[group],
            send_sem=send_sem.at[target],
            recv_sem=recv_sem.at[group],
            device_id={"grp": target},
            device_id_type=MESH,
        )

    def received(buffer_out, buffer_in, send_sem, recv_sem, source):
        return pltpu.make_async_remote_copy(
            src_ref=buffer_out.at[source],
            dst_ref=buffer_in.at[source],
            send_sem=send_sem.at[source],
            recv_sem=recv_sem.at[source],
            device_id={"grp": source},
            device_id_type=MESH,
        )

    gram_set = (gram_out, gram_in, gram_send, gram_recv)
    rows_set = (rows_out, rows_in, rows_send, rows_recv)
    code_set = (code_out, code_in, code_send, code_recv)

    def start_all(buffers):
        def one(step, carry):
            send_to(*buffers, lax.rem(group + step, groups)).start()
            return carry

        lax.fori_loop(1, groups, one, 0)

    def wait_all(buffers, way):
        def one(step, carry):
            copy = received(*buffers, lax.rem(group + step, groups))
            if way == "recv":
                copy.wait_recv()
            else:
                copy.wait_send()
            return carry

        lax.fori_loop(1, groups, one, 0)

    def encode(owner, carry):
        low, high = jnp.int32(NONE), jnp.int32(-1)
        for j in range(slots):
            offset = places[j] - owner * OWNED
            mine = (offset >= 0) & (offset < OWNED)
            low = jnp.minimum(low, jnp.where(mine, offset, NONE))
            high = jnp.maximum(high, jnp.where(mine, offset, -1))
        high = jnp.where(high > low, high, NONE)
        lows[owner] = low
        highs[owner] = high
        code_out[owner] = jnp.where(code_row == 0, low, high)
        return carry

    lax.fori_loop(0, groups, encode, 0)
    start_all(code_set)

    def ring_step(step, carry):
        for mode in range(3):
            for way in range(2):
                hop(way, step - 1, mode, arrived(way, step - 1)).wait_recv()
                hop(way, step, mode, sent(way, step)).start()
        return carry

    lax.fori_loop(1, half_way - 1, ring_step, 0)
    end = half_way - 1
    for mode in range(3):
        for way in range(2):
            hop(way, end - 1, mode, arrived(way, end - 1)).wait_recv()
            if way == last_way(mode):
                hop(way, end, mode, sent(way, end)).start()
    for mode in range(3):
        way = last_way(mode)
        hop(way, end, mode, arrived(way, end)).wait_recv()

    height = R // groups
    for mode in range(3):
        factor = table[mode].reshape(owned * members * B, R)
        gram = lax.dot_general(
            factor, factor, (((0,), (0,)), ((), ())), preferred_element_type=jnp.float32
        )
        gram_out[:, mode] = gram.reshape(groups, height, R)
    start_all(gram_set)
    load.wait()

    def one_slot(j, carry):
        third = table[1, coords_ref[2, j]].astype(jnp.float32)
        fourth = table[2, coords_ref[3, j]].astype(jnp.float32)
        khatri = (third[:, None, :] * fourth[None, :, :]).reshape(B * B, R).astype(jnp.bfloat16)
        product = jnp.dot(blocks[j], khatri, preferred_element_type=jnp.float32)
        second = table[0, coords_ref[1, j]].astype(jnp.float32)
        parts[j] = jnp.sum(product.reshape(B, B, R) * second[None, :, :], axis=1)
        return carry

    lax.fori_loop(0, slots, one_slot, 0)

    def pack(owner, carry):
        values = [parts[j] for j in range(slots)]
        for slot, chosen in enumerate((lows[owner], highs[owner])):
            total = jnp.zeros((B, R), jnp.float32)
            for j in range(slots):
                total = total + jnp.where(places[j] - owner * OWNED == chosen, values[j], 0.0)
            rows_out[owner, slot] = total.astype(jnp.bfloat16)
        return carry

    lax.fori_loop(0, groups, pack, 0)

    wait_all(gram_set, "recv")

    def add_gram(step, total):
        return total + gram_in[lax.rem(group + step, groups)]

    total = lax.fori_loop(1, groups, add_gram, gram_out[group])
    system[group] = total[0] * total[1] * total[2]

    def system_copy(index, target):
        return pltpu.make_async_remote_copy(
            src_ref=system.at[index],
            dst_ref=system.at[index],
            send_sem=system_send.at[target],
            recv_sem=system_recv.at[index],
            device_id={"grp": target},
            device_id_type=MESH,
        )

    def system_start(step, carry):
        system_copy(group, lax.rem(group + step, groups)).start()
        return carry

    lax.fori_loop(1, groups, system_start, 0)
    start_all(rows_set)

    def system_wait(step, carry):
        other = lax.rem(group + step, groups)
        system_copy(other, other).wait_recv()
        return carry

    lax.fori_loop(1, groups, system_wait, 0)
    system_ref[...] = system[...].reshape(R, R)

    wait_all(code_set, "recv")
    wait_all(rows_set, "recv")
    rows_in[group] = rows_out[group]
    code_in[group] = code_out[group]

    def add_rows(source, totals):
        code = code_in[source]
        for slot in range(2):
            values = rows_in[source, slot].astype(jnp.float32)
            place = jnp.broadcast_to(code[slot : slot + 1], (B, R))
            totals = tuple(
                t + jnp.where(place == p, values, 0.0) for p, t in enumerate(totals)
            )
        return totals

    totals = lax.fori_loop(0, groups, add_rows, (jnp.zeros((B, R), jnp.float32),) * OWNED)
    for p in range(OWNED):
        sums_ref[p * B : (p + 1) * B, :] = totals[p]

    wait_all(code_set, "send")
    wait_all(gram_set, "send")
    wait_all(rows_set, "send")

    def system_sent(step, carry):
        other = lax.rem(group + step, groups)
        system_copy(group, other).wait_send()
        return carry

    lax.fori_loop(1, groups, system_sent, 0)

    def ring_sent(step, carry):
        for mode in range(3):
            for way in range(2):
                hop(way, step, mode, sent(way, step)).wait_send()
        return carry

    lax.fori_loop(0, end, ring_sent, 0)
    for mode in range(3):
        way = last_way(mode)
        hop(way, end, mode, sent(way, end)).wait_send()


def on_device(
    tensor_blocks, block_coords, live_count, owner_order, factor_two, factor_three, factor_four
):
    groups = lax.axis_size("grp")
    members = lax.axis_size("mem")
    slots = tensor_blocks.shape[0]
    owned = factor_two.shape[0] // B
    height = R // groups
    smem = pl.BlockSpec(memory_space=pltpu.SMEM)
    vmem = pl.BlockSpec(memory_space=pltpu.VMEM)
    dma = pltpu.SemaphoreType.DMA
    system, sums = pl.pallas_call(
        functools.partial(gather_kernel, groups, members),
        out_shape=(
            jax.ShapeDtypeStruct((R, R), jnp.float32),
            jax.ShapeDtypeStruct((OWNED * B, R), jnp.float32),
        ),
        in_specs=[smem, smem, smem, pl.BlockSpec(memory_space=pl.ANY), vmem, vmem, vmem],
        out_specs=(vmem, vmem),
        scratch_shapes=[
            pltpu.VMEM(tensor_blocks.shape, jnp.bfloat16),
            pltpu.VMEM((3, members * owned, B, R), jnp.bfloat16),
            pltpu.VMEM((slots, B, R), jnp.float32),
            pltpu.VMEM((groups, 3, height, R), jnp.float32),
            pltpu.VMEM((groups, 3, height, R), jnp.float32),
            pltpu.VMEM((groups, height, R), jnp.float32),
            pltpu.VMEM((groups, 2, B, R), jnp.bfloat16),
            pltpu.VMEM((groups, 2, B, R), jnp.bfloat16),
            pltpu.VMEM((groups, 8, R), jnp.int32),
            pltpu.VMEM((groups, 8, R), jnp.int32),
            pltpu.SMEM((groups,), jnp.int32),
            pltpu.SMEM((groups,), jnp.int32),
            dma,
            dma((2, members // 2, 3)),
            dma((2, members // 2, 3)),
        ]
        + [dma((groups,))] * 8,
        compiler_params=pltpu.CompilerParams(
            collective_id=0, has_side_effects=True, vmem_limit_bytes=40 << 20
        ),
        name="gather_rows",
    )(
        block_coords,
        live_count,
        owner_order,
        tensor_blocks,
        factor_two,
        factor_three,
        factor_four,
    )
    return solve_rows(system, sums)[None]


def solution(mesh):
    return jax.shard_map(
        on_device,
        mesh=mesh,
        in_specs=(
            P(("grp", "mem"), None, None),
            P(None, ("grp", "mem")),
            P("grp", "mem"),
            P("mem", None),
            P(("grp", "mem"), None),
            P(("grp", "mem"), None),
            P(("grp", "mem"), None),
        ),
        out_specs=P("mem", "grp", None),
        check_vma=False,
    )
```

time: 2240 us -> 83.5 us (0.04); the launches traced: 2200 us -> 83 us
  local copies, waits for them, and re-layouts: 716 us -> 5.36 us
  matrix products: 478 us -> 0 us
  waiting for transfers between devices: 375 us -> 0 us
  loops' own time: 367 us -> 0 us
  other arithmetic: 165 us -> 0 us
  blocking collectives: 82.3 us -> 0 us
  Pallas kernels: 0 us -> 77 us
    dynamic_slice x1286 -> x0, local copies, waits for them, and re-layouts: 491 us -> none  [the longest x256 166 us: column(): corner = lax.dynamic_index_in_dim(target, step, 0, keepdims=False)]
    dot_general x775 -> x0, matrix products: 478 us -> none  [the longest x256 201 us: backward(): jnp.dot(solved, col_now, precision=lax.Precision.HIGHEST)]
    psum x1 -> x0, waiting for transfers between devices: 375 us -> none  [on_device(): lax.psum((gram_matrix(factor_two), gram_matrix(factor_three), gram_matrix...]
    another operation x4 -> x0, loops' own time: 367 us -> none  [the longest x1 355 us: cholesky_lower(): lax.fori_loop(jnp.int32(0), jnp.int32(size), column, jnp.zeros_like(system))]
    dynamic_update_slice x768 -> x0, local copies, waits for them, and re-layouts: 176 us -> none  [the longest x256 157 us: column(): return lax.dynamic_update_index_in_dim(lower, values[:, None], step, 1)]
    dot_general x256 -> x0, other arithmetic: 161 us -> none  [column(): jnp.dot(row_now, row_now, precision=lax.Precision.HIGHEST)]
    all_gather x3 -> x0, blocking collectives: 82.3 us -> none  [the longest x1 33.4 us: on_device(): lax.all_gather(factor_three, 'mem', axis=0, tiled=True)]
    pallas_call x0 -> x2, Pallas kernels: none -> 77 us  [the longest x1 66.4 us: on_device(): pl.pallas_call(functools.partial(gather_kernel, groups, members), out_sha...]
  transfers between devices with their start and end apart: 2 -> 0, of which waited for: 1 -> 0; matrix products, arithmetic and copies ran while one was open for 28% -> 0% of each run, Pallas kernels for 0% -> 0%
where the time goes in v1:
time: 83.5 us; the launch traced here: 83 us
  Pallas kernels  77 us (92%)
  local copies, waits for them, and re-layouts  5.36 us (6%)
    pallas_call x1, Pallas kernels, on_device(): pl.pallas_call(functools.partial(gather_kernel, groups, members), out_sha...  66.4 us
    pallas_call x1, Pallas kernels, solve_rows(): pl.pallas_call(solve_kernel, out_shape=jax.ShapeDtypeStruct(sums.shape, j...  10.6 us
    unnamed x16, local copies, waits for them, and re-layouts  5.36 us

profile of v1, /device:TPU:1, one launch (start us, length us, event | category | flops | bytes accessed | tf_op | source)
XLA Modules:
  0.0 83.0 jit_solution(15195870551097715447)
XLA Ops:
  0.0 0.0 copy-start.7
  0.7 0.0 copy-done.7
  0.7 0.0 copy-start
  0.7 1.2 %copy-done = bf16[8,256,256]{2,1,0:T(8,128)(2,1)S(1)} copy-done((bf16[8,256,256]{2,1,0:T(8,128)(2,1)S(1)}, bf16[8,256,256]{2,1,0:T(8,128)(2,1)}, u32[]{:S(2)}) %copy-start) | copy-done | bytes 1048600
  1.9 0.0 copy-start.3
  1.9 0.7 copy-done.3
  2.6 0.0 copy-start.4
  2.6 0.7 copy-done.4
  3.3 0.0 copy-start.5
  3.3 0.7 copy-done.5
  4.1 0.0 copy-start.6
  4.1 0.7 copy-done.6
  4.7 66.4 %gather_rows.1 = (f32[256,256]{1,0:T(8,128)S(1)}, f32[64,256]{1,0:T(8,128)S(1)}) custom-call(s32[4,8]{1,0:T(4,128)S(1)} %copy-done.6, s32[1,1]{1,0:T(1,128)S(6)} %copy.8.live_ref, s32[1,128]{1,0:T(1,128)S(1)} %copy-done.7, bf16[8,256,256]{2,1,0:T(8,128)(2,1)S(1)} %copy-done, bf16[32,256]{1,0:T(8,128)(2,1)S(1)} %copy-done.3, bf16[32,256]{1,0:T(8,128)(2,1)S(1)} %copy-done.4, ...), custom_call_target="tpu_custom_call" | custom-call | tf_op jit(solution)/shard_map/gather_rows/pallas_call | solution.py:384
  71.2 0.0 copy-start.1
  71.2 0.7 copy-done.1
  71.8 0.0 copy-start.2
  71.8 0.6 copy-done.2
  72.5 10.6 %solve_rows.1 = f32[64,256]{1,0:T(8,128)} custom-call(f32[256,256]{1,0:T(8,128)} %copy-done.1, f32[64,256]{1,0:T(8,128)} %copy-done.2), custom_call_target="tpu_custom_call" | custom-call | tf_op jit(solution)/shard_map/solve_rows/pallas_call | solution.py:79
Async XLA Ops:
  0.0 0.7 copy-start.7
  0.7 1.2 %copy-start = (bf16[8,256,256]{2,1,0:T(8,128)(2,1)S(1)}, bf16[8,256,256]{2,1,0:T(8,128)(2,1)}, u32[]{:S(2)}) copy-start(bf16[8,256,256]{2,1,0:T(8,128)(2,1)} %blocks_ref.1) | copy-start | bytes 3145732
  1.9 0.7 copy-start.3
  2.6 0.7 copy-start.4
  3.3 0.7 copy-start.5
  4.1 0.7 copy-start.6
  71.2 0.7 copy-start.1
  71.8 0.6 copy-start.2

commit v2 on v1

--- a/solution.py
+++ b/solution.py
@@ -61,41 +61,20 @@
                 ref[at : at + 8, :] = part
 
 
-def solve_kernel(system_ref, sums_ref, out_ref, first_ref, second_ref):
-    first_ref[...] = system_ref[0:HALF, 0:HALF]
-    invert_half(first_ref)
-    first = first_ref[...]
-    cross = system_ref[0:HALF, HALF:R]
-    weights = dot_full(first, cross)
-    second_ref[...] = system_ref[HALF:R, HALF:R] - dot_full(cross, weights, 0, 0)
-    left = sums_ref[:, 0:HALF]
-    invert_half(second_ref)
-    right = dot_full(sums_ref[:, HALF:R] - dot_full(left, weights), second_ref[...])
-    out_ref[:, HALF:R] = right
-    out_ref[:, 0:HALF] = dot_full(left, first) - dot_full(right, weights, 1, 1)
-
-
-def solve_rows(system, sums):
-    return pl.pallas_call(
-        solve_kernel,
-        out_shape=jax.ShapeDtypeStruct(sums.shape, jnp.float32),
-        scratch_shapes=[pltpu.VMEM((HALF, HALF), jnp.float32)] * 2,
-        name="solve_rows",
-    )(system, sums)
-
-
-def gather_kernel(
+def update_kernel(
     groups,
     members,
+    coords_hbm,
+    live_hbm,
+    order_hbm,
+    blocks_hbm,
+    two_hbm,
+    three_hbm,
+    four_hbm,
+    out_ref,
     coords_ref,
     live_ref,
     order_ref,
-    blocks_ref,
-    two_ref,
-    three_ref,
-    four_ref,
-    system_ref,
-    sums_ref,
     blocks,
     table,
     parts,
@@ -108,7 +87,9 @@
     code_in,
     lows,
     highs,
-    block_sem,
+    first_ref,
+    second_ref,
+    load_sem,
     ring_send,
     ring_recv,
     gram_send,
@@ -123,17 +104,31 @@
     group = lax.axis_index("grp")
     member = lax.axis_index("mem")
     slots = blocks.shape[0]
-    owned = two_ref.shape[0] // B
-    half_way = members // 2
-    after = lax.rem(member + 1, members)
-    before = lax.rem(member + members - 1, members)
-
-    load = pltpu.make_async_copy(blocks_ref, blocks, block_sem)
-    load.start()
+    owned = two_hbm.shape[0]
+
+    def beside(shift):
+        return lax.rem(member + members + shift, members)
+
+
+    factor_loads = [
+        pltpu.make_async_copy(
+            ref, table.at[mode, pl.ds(member * owned, owned)], load_sem.at[mode]
+        )
+        for mode, ref in enumerate((two_hbm, three_hbm, four_hbm))
+    ]
+    index_loads = [
+        pltpu.make_async_copy(ref, to, load_sem.at[3 + i])
+        for i, (ref, to) in enumerate(
+            ((coords_hbm, coords_ref), (live_hbm, live_ref), (order_hbm, order_ref))
+        )
+    ]
+    load = pltpu.make_async_copy(blocks_hbm, blocks, load_sem.at[6])
+    for copy in factor_loads + index_loads + [load]:
+        copy.start()
 
     barrier = pltpu.get_barrier_semaphore()
-    for neighbour in (after, before):
-        pl.semaphore_signal(barrier, inc=1, device_id={"mem": neighbour}, device_id_type=MESH)
+    for shift in (1, 2, -1, -2):
+        pl.semaphore_signal(barrier, inc=1, device_id={"mem": beside(shift)}, device_id_type=MESH)
 
     def greet(step, carry):
         pl.semaphore_signal(
@@ -145,36 +140,50 @@
         return carry
 
     lax.fori_loop(1, groups, greet, 0)
-    for mode, ref in enumerate((two_ref, three_ref, four_ref)):
-        for i in range(owned):
-            table[mode, member * owned + i] = ref[i * B : (i + 1) * B, :]
-    pl.semaphore_wait(barrier, groups + 1)
-
-    def hop(way, step, mode, source):
-        chunk = table.at[mode, pl.ds(source * owned, owned)]
+    for copy in factor_loads:
+        copy.wait()
+    pl.semaphore_wait(barrier, groups + 3)
+
+    reach = (members // 2, members // 2 - 1)
+    sign = (1, -1)
+
+    def travel(way, distance, step, mode):
+        chunk = table.at[mode, pl.ds(beside(-sign[way] * distance) * owned, owned)]
         return pltpu.make_async_remote_copy(
             src_ref=chunk,
             dst_ref=chunk,
-            send_sem=ring_send.at[way, step, mode],
-            recv_sem=ring_recv.at[way, step, mode],
-            device_id={"mem": after if way == 0 else before},
-            device_id_type=MESH,
-        )
-
-    def sent(way, step):
-        shift = step if way == 1 else members - step
-        return lax.rem(member + shift, members)
-
-    def arrived(way, step):
-        shift = step + 1 if way == 1 else members - step - 1
-        return lax.rem(member + shift, members)
-
-    def last_way(mode):
-        return 0 if mode < 2 else 1
-
-    for mode in range(3):
-        for way in range(2):
-            hop(way, 0, mode, sent(way, 0)).start()
+            send_sem=ring_send.at[way, distance + step - 1, mode],
+            recv_sem=ring_recv.at[way, distance + step - 1, mode],
+            device_id={"mem": beside(sign[way] * step)},
+            device_id_type=MESH,
+        )
+
+    def arrival(way, distance, mode):
+        chunk = table.at[mode, pl.ds(beside(-sign[way] * distance) * owned, owned)]
+        return pltpu.make_async_remote_copy(
+            src_ref=chunk,
+            dst_ref=chunk,
+            send_sem=ring_send.at[way, distance - 1, mode],
+            recv_sem=ring_recv.at[way, distance - 1, mode],
+            device_id={"mem": beside(-sign[way])},
+            device_id_type=MESH,
+        )
+
+    def relay(distance):
+        for mode in range(3):
+            for way in range(2):
+                if 0 < distance <= reach[way]:
+                    arrival(way, distance, mode).wait_recv()
+                if distance + 2 <= reach[way]:
+                    travel(way, distance, 2, mode).start()
+        for mode in range(3):
+            for way in range(2):
+                if distance + 1 <= reach[way]:
+                    travel(way, distance, 1, mode).start()
+
+    relay(0)
+    for copy in index_loads:
+        copy.wait()
 
     live = live_ref[0, 0]
     wanted = [coords_ref[0, j] for j in range(slots)]
@@ -218,13 +227,12 @@
 
         lax.fori_loop(1, groups, one, 0)
 
-    def wait_all(buffers, way):
+    def from_other(step):
+        return lax.rem(group + groups - step, groups)
+
+    def wait_sent(buffers):
         def one(step, carry):
-            copy = received(*buffers, lax.rem(group + step, groups))
-            if way == "recv":
-                copy.wait_recv()
-            else:
-                copy.wait_send()
+            received(*buffers, lax.rem(group + step, groups)).wait_send()
             return carry
 
         lax.fori_loop(1, groups, one, 0)
@@ -245,23 +253,13 @@
     lax.fori_loop(0, groups, encode, 0)
     start_all(code_set)
 
-    def ring_step(step, carry):
+    for distance in range(2, reach[0] + 1, 2):
+        relay(distance)
+    for distance in range(1, reach[0] + 1, 2):
         for mode in range(3):
             for way in range(2):
-                hop(way, step - 1, mode, arrived(way, step - 1)).wait_recv()
-                hop(way, step, mode, sent(way, step)).start()
-        return carry
-
-    lax.fori_loop(1, half_way - 1, ring_step, 0)
-    end = half_way - 1
-    for mode in range(3):
-        for way in range(2):
-            hop(way, end - 1, mode, arrived(way, end - 1)).wait_recv()
-            if way == last_way(mode):
-                hop(way, end, mode, sent(way, end)).start()
-    for mode in range(3):
-        way = last_way(mode)
-        hop(way, end, mode, arrived(way, end)).wait_recv()
+                if distance <= reach[way]:
+                    arrival(way, distance, mode).wait_recv()
 
     height = R // groups
     for mode in range(3):
@@ -295,10 +293,10 @@
 
     lax.fori_loop(0, groups, pack, 0)
 
-    wait_all(gram_set, "recv")
-
     def add_gram(step, total):
-        return total + gram_in[lax.rem(group + step, groups)]
+        source = from_other(step)
+        received(*gram_set, source).wait_recv()
+        return total + gram_in[source]
 
     total = lax.fori_loop(1, groups, add_gram, gram_out[group])
     system[group] = total[0] * total[1] * total[2]
@@ -321,35 +319,48 @@
     start_all(rows_set)
 
     def system_wait(step, carry):
-        other = lax.rem(group + step, groups)
+        other = from_other(step)
         system_copy(other, other).wait_recv()
         return carry
 
     lax.fori_loop(1, groups, system_wait, 0)
-    system_ref[...] = system[...].reshape(R, R)
-
-    wait_all(code_set, "recv")
-    wait_all(rows_set, "recv")
-    rows_in[group] = rows_out[group]
-    code_in[group] = code_out[group]
-
-    def add_rows(source, totals):
-        code = code_in[source]
+    first_ref[...] = system[0 : groups // 2].reshape(HALF, R)[:, 0:HALF]
+    invert_half(first_ref)
+    first = first_ref[...]
+    cross = system[0 : groups // 2].reshape(HALF, R)[:, HALF:R]
+    weights = dot_full(first, cross)
+    second_ref[...] = system[groups // 2 :].reshape(HALF, R)[:, HALF:R] - dot_full(
+        cross, weights, 0, 0
+    )
+    invert_half(second_ref)
+
+    def add_code(code, rows, totals):
         for slot in range(2):
-            values = rows_in[source, slot].astype(jnp.float32)
+            values = rows[slot].astype(jnp.float32)
             place = jnp.broadcast_to(code[slot : slot + 1], (B, R))
             totals = tuple(
                 t + jnp.where(place == p, values, 0.0) for p, t in enumerate(totals)
             )
         return totals
 
-    totals = lax.fori_loop(0, groups, add_rows, (jnp.zeros((B, R), jnp.float32),) * OWNED)
-    for p in range(OWNED):
-        sums_ref[p * B : (p + 1) * B, :] = totals[p]
-
-    wait_all(code_set, "send")
-    wait_all(gram_set, "send")
-    wait_all(rows_set, "send")
+    def add_rows(step, totals):
+        source = from_other(step)
+        received(*code_set, source).wait_recv()
+        received(*rows_set, source).wait_recv()
+        return add_code(code_in[source], rows_in[source], totals)
+
+    totals = (jnp.zeros((B, R), jnp.float32),) * OWNED
+    totals = add_code(code_out[group], rows_out[group], totals)
+    totals = lax.fori_loop(1, groups, add_rows, totals)
+    sums = jnp.concatenate(totals, axis=0)
+    left = sums[:, 0:HALF]
+    right = dot_full(sums[:, HALF:R] - dot_full(left, weights), second_ref[...])
+    out_ref[:, HALF:R] = right
+    out_ref[:, 0:HALF] = dot_full(left, first) - dot_full(right, weights, 1, 1)
+
+    wait_sent(code_set)
+    wait_sent(gram_set)
+    wait_sent(rows_set)
 
     def system_sent(step, carry):
         other = lax.rem(group + step, groups)
@@ -358,16 +369,11 @@
 
     lax.fori_loop(1, groups, system_sent, 0)
 
-    def ring_sent(step, carry):
+    for distance in range(1, reach[0] + 1):
         for mode in range(3):
             for way in range(2):
-                hop(way, step, mode, sent(way, step)).wait_send()
-        return carry
-
-    lax.fori_loop(0, end, ring_sent, 0)
-    for mode in range(3):
-        way = last_way(mode)
-        hop(way, end, mode, sent(way, end)).wait_send()
+                if distance <= reach[way]:
+                    arrival(way, distance, mode).wait_send()
 
 
 def on_device(
@@ -378,18 +384,19 @@
     slots = tensor_blocks.shape[0]
     owned = factor_two.shape[0] // B
     height = R // groups
-    smem = pl.BlockSpec(memory_space=pltpu.SMEM)
+    hbm = pl.BlockSpec(memory_space=pl.ANY)
     vmem = pl.BlockSpec(memory_space=pltpu.VMEM)
     dma = pltpu.SemaphoreType.DMA
-    system, sums = pl.pallas_call(
-        functools.partial(gather_kernel, groups, members),
-        out_shape=(
-            jax.ShapeDtypeStruct((R, R), jnp.float32),
-            jax.ShapeDtypeStruct((OWNED * B, R), jnp.float32),
-        ),
-        in_specs=[smem, smem, smem, pl.BlockSpec(memory_space=pl.ANY), vmem, vmem, vmem],
-        out_specs=(vmem, vmem),
+    factors = [f.reshape(owned, B, R) for f in (factor_two, factor_three, factor_four)]
+    solved = pl.pallas_call(
+        functools.partial(update_kernel, groups, members),
+        out_shape=jax.ShapeDtypeStruct((OWNED * B, R), jnp.float32),
+        in_specs=[hbm] * 7,
+        out_specs=vmem,
         scratch_shapes=[
+            pltpu.SMEM(block_coords.shape, jnp.int32),
+            pltpu.SMEM(live_count.shape, jnp.int32),
+            pltpu.SMEM(owner_order.shape, jnp.int32),
             pltpu.VMEM(tensor_blocks.shape, jnp.bfloat16),
             pltpu.VMEM((3, members * owned, B, R), jnp.bfloat16),
             pltpu.VMEM((slots, B, R), jnp.float32),
@@ -402,25 +409,19 @@
             pltpu.VMEM((groups, 8, R), jnp.int32),
             pltpu.SMEM((groups,), jnp.int32),
             pltpu.SMEM((groups,), jnp.int32),
-            dma,
+            pltpu.VMEM((HALF, HALF), jnp.float32),
+            pltpu.VMEM((HALF, HALF), jnp.float32),
+            dma((7,)),
             dma((2, members // 2, 3)),
             dma((2, members // 2, 3)),
         ]
         + [dma((groups,))] * 8,
         compiler_params=pltpu.CompilerParams(
-            collective_id=0, has_side_effects=True, vmem_limit_bytes=40 << 20
+            collective_id=0, has_side_effects=True, vmem_limit_bytes=60 << 20
         ),
-        name="gather_rows",
-    )(
-        block_coords,
-        live_count,
-        owner_order,
-        tensor_blocks,
-        factor_two,
-        factor_three,
-        factor_four,
-    )
-    return solve_rows(system, sums)[None]
+        name="update_rows",
+    )(block_coords, live_count, owner_order, tensor_blocks, *factors)
+    return solved[None]
 
 
 def solution(mesh):

time: 83.5 us -> 66.4 us (0.80)
  Pallas kernels: 77 us -> 64.1 us
  local copies, waits for them, and re-layouts: 5.36 us -> 1.47 us
    pallas_call x2 -> x1, Pallas kernels: 77 us -> 64.1 us  [on_device(): pl.pallas_call(functools.partial(update_kernel, groups, members), out_sha...]
    unnamed x16 -> x1, local copies, waits for them, and re-layouts: 5.36 us -> 1.47 us
where the time goes in v2:
time: 66.4 us; the launch traced here: 66.2 us
  Pallas kernels  64.1 us (97%)
  local copies, waits for them, and re-layouts  1.47 us (2%)
    pallas_call x1, Pallas kernels, on_device(): pl.pallas_call(functools.partial(update_kernel, groups, members), out_sha...  64.1 us
    unnamed x1, local copies, waits for them, and re-layouts  1.47 us

profile of v2, /device:TPU:1, one launch (start us, length us, event | category | flops | bytes accessed | tf_op | source)
XLA Modules:
  0.0 66.2 jit_solution(8812175586780398581)
XLA Ops:
  0.7 64.1 %update_rows.1 = f32[64,256]{1,0:T(8,128)} custom-call(s32[4,8]{1,0:T(4,128)} %coords_hbm.1, s32[1,1]{1,0:T(1,128)S(6)} %copy.9.live_hbm, s32[1,128]{1,0:T(1,128)} %order_hbm.1, bf16[8,256,256]{2,1,0:T(8,128)(2,1)} %blocks_hbm.1, bf16[2,16,256]{2,1,0:T(8,128)(2,1)} %bitcast.5, bf16[2,16,256]{2,1,0:T(8,128)(2,1)} %bitcast.6, bf16[2,16,256]{2,1,0:T(8,128)(2,1)} %bitcast.7), custom_call_target="tpu_custom_call" | custom-call | tf_op jit(solution)/shard_map/update_rows/pallas_call | solution.py:391
  64.7 1.5 %copy.10 = f32[1,64,256]{2,1,0:T(8,128)} copy(f32[1,64,256]{2,1,0:T(8,128)} %bitcast.4) | data formatting | bytes 131072

commit v3 on v2

--- a/solution.py
+++ b/solution.py
@@ -139,7 +139,7 @@
         )
         return carry
 
-    lax.fori_loop(1, groups, greet, 0)
+    lax.fori_loop(1, groups, greet, 0, unroll=True)
     for copy in factor_loads:
         copy.wait()
     pl.semaphore_wait(barrier, groups + 3)
@@ -152,7 +152,7 @@
         return pltpu.make_async_remote_copy(
             src_ref=chunk,
             dst_ref=chunk,
-            send_sem=ring_send.at[way, distance + step - 1, mode],
+            send_sem=ring_send,
             recv_sem=ring_recv.at[way, distance + step - 1, mode],
             device_id={"mem": beside(sign[way] * step)},
             device_id_type=MESH,
@@ -163,7 +163,7 @@
         return pltpu.make_async_remote_copy(
             src_ref=chunk,
             dst_ref=chunk,
-            send_sem=ring_send.at[way, distance - 1, mode],
+            send_sem=ring_send,
             recv_sem=ring_recv.at[way, distance - 1, mode],
             device_id={"mem": beside(-sign[way])},
             device_id_type=MESH,
@@ -194,27 +194,21 @@
 
     found = lax.fori_loop(0, groups * OWNED, find, (jnp.int32(0),) * slots, unroll=4)
     places = [jnp.where(j < live, found[j], -NONE) for j in range(slots)]
-    code_row = lax.broadcasted_iota(jnp.int32, (8, R), 0)
+    code_row = lax.broadcasted_iota(jnp.int32, (8, HALF), 0)
 
     def send_to(buffer_out, buffer_in, send_sem, recv_sem, target):
         return pltpu.make_async_remote_copy(
             src_ref=buffer_out.at[target],
             dst_ref=buffer_in.at[group],
-            send_sem=send_sem.at[target],
-            recv_sem=recv_sem.at[group],
+            send_sem=send_sem,
+            recv_sem=recv_sem,
             device_id={"grp": target},
             device_id_type=MESH,
         )
 
-    def received(buffer_out, buffer_in, send_sem, recv_sem, source):
-        return pltpu.make_async_remote_copy(
-            src_ref=buffer_out.at[source],
-            dst_ref=buffer_in.at[source],
-            send_sem=send_sem.at[source],
-            recv_sem=recv_sem.at[source],
-            device_id={"grp": source},
-            device_id_type=MESH,
-        )
+    def wait_others(buffer, sem):
+        others = buffer.at[pl.ds(0, groups - 1)]
+        pltpu.make_async_copy(others, others, sem).wait()
 
     gram_set = (gram_out, gram_in, gram_send, gram_recv)
     rows_set = (rows_out, rows_in, rows_send, rows_recv)
@@ -225,17 +219,10 @@
             send_to(*buffers, lax.rem(group + step, groups)).start()
             return carry
 
-        lax.fori_loop(1, groups, one, 0)
+        lax.fori_loop(1, groups, one, 0, unroll=True)
 
     def from_other(step):
         return lax.rem(group + groups - step, groups)
-
-    def wait_sent(buffers):
-        def one(step, carry):
-            received(*buffers, lax.rem(group + step, groups)).wait_send()
-            return carry
-
-        lax.fori_loop(1, groups, one, 0)
 
     def encode(owner, carry):
         low, high = jnp.int32(NONE), jnp.int32(-1)
@@ -253,16 +240,16 @@
     lax.fori_loop(0, groups, encode, 0)
     start_all(code_set)
 
-    for distance in range(2, reach[0] + 1, 2):
+    for distance in range(2, reach[0], 2):
         relay(distance)
-    for distance in range(1, reach[0] + 1, 2):
-        for mode in range(3):
+    height = R // groups
+    for mode in range(3):
+        for distance in range(1, reach[0] + 1, 2):
             for way in range(2):
                 if distance <= reach[way]:
                     arrival(way, distance, mode).wait_recv()
-
-    height = R // groups
-    for mode in range(3):
+        if reach[0] % 2 == 0:
+            arrival(0, reach[0], mode).wait_recv()
         factor = table[mode].reshape(owned * members * B, R)
         gram = lax.dot_general(
             factor, factor, (((0,), (0,)), ((), ())), preferred_element_type=jnp.float32
@@ -293,20 +280,20 @@
 
     lax.fori_loop(0, groups, pack, 0)
 
+    wait_others(gram_in, gram_recv)
+
     def add_gram(step, total):
-        source = from_other(step)
-        received(*gram_set, source).wait_recv()
-        return total + gram_in[source]
-
-    total = lax.fori_loop(1, groups, add_gram, gram_out[group])
+        return total + gram_in[from_other(step)]
+
+    total = lax.fori_loop(1, groups, add_gram, gram_out[group], unroll=True)
     system[group] = total[0] * total[1] * total[2]
 
     def system_copy(index, target):
         return pltpu.make_async_remote_copy(
             src_ref=system.at[index],
             dst_ref=system.at[index],
-            send_sem=system_send.at[target],
-            recv_sem=system_recv.at[index],
+            send_sem=system_send,
+            recv_sem=system_recv,
             device_id={"grp": target},
             device_id_type=MESH,
         )
@@ -315,15 +302,14 @@
         system_copy(group, lax.rem(group + step, groups)).start()
         return carry
 
-    lax.fori_loop(1, groups, system_start, 0)
+    lax.fori_loop(1, groups, system_start, 0, unroll=True)
     start_all(rows_set)
 
-    def system_wait(step, carry):
-        other = from_other(step)
-        system_copy(other, other).wait_recv()
-        return carry
-
-    lax.fori_loop(1, groups, system_wait, 0)
+    passed = table.at[:, pl.ds(0, (reach[0] + reach[1]) * owned)]
+    pltpu.make_async_copy(passed, passed, ring_send).wait()
+    wait_others(gram_out, gram_send)
+    wait_others(code_out, code_send)
+    wait_others(system, system_recv)
     first_ref[...] = system[0 : groups // 2].reshape(HALF, R)[:, 0:HALF]
     invert_half(first_ref)
     first = first_ref[...]
@@ -332,12 +318,11 @@
     second_ref[...] = system[groups // 2 :].reshape(HALF, R)[:, HALF:R] - dot_full(
         cross, weights, 0, 0
     )
-    invert_half(second_ref)
-
     def add_code(code, rows, totals):
         for slot in range(2):
             values = rows[slot].astype(jnp.float32)
-            place = jnp.broadcast_to(code[slot : slot + 1], (B, R))
+            place = jnp.broadcast_to(code[slot : slot + 1], (B, HALF))
+            place = jnp.concatenate([place, place], axis=1)
             totals = tuple(
                 t + jnp.where(place == p, values, 0.0) for p, t in enumerate(totals)
             )
@@ -345,35 +330,24 @@
 
     def add_rows(step, totals):
         source = from_other(step)
-        received(*code_set, source).wait_recv()
-        received(*rows_set, source).wait_recv()
         return add_code(code_in[source], rows_in[source], totals)
 
     totals = (jnp.zeros((B, R), jnp.float32),) * OWNED
     totals = add_code(code_out[group], rows_out[group], totals)
-    totals = lax.fori_loop(1, groups, add_rows, totals)
+    wait_others(code_in, code_recv)
+    wait_others(rows_in, rows_recv)
+    wait_others(system, system_send)
+    wait_others(rows_out, rows_send)
+    totals = lax.fori_loop(1, groups, add_rows, totals, unroll=4)
     sums = jnp.concatenate(totals, axis=0)
     left = sums[:, 0:HALF]
-    right = dot_full(sums[:, HALF:R] - dot_full(left, weights), second_ref[...])
+    right = sums[:, HALF:R] - dot_full(left, weights)
+    left = dot_full(left, first)
+    invert_half(second_ref)
+    right = dot_full(right, second_ref[...])
+
     out_ref[:, HALF:R] = right
-    out_ref[:, 0:HALF] = dot_full(left, first) - dot_full(right, weights, 1, 1)
-
-    wait_sent(code_set)
-    wait_sent(gram_set)
-    wait_sent(rows_set)
-
-    def system_sent(step, carry):
-        other = lax.rem(group + step, groups)
-        system_copy(group, other).wait_send()
-        return carry
-
-    lax.fori_loop(1, groups, system_sent, 0)
-
-    for distance in range(1, reach[0] + 1):
-        for mode in range(3):
-            for way in range(2):
-                if distance <= reach[way]:
-                    arrival(way, distance, mode).wait_send()
+    out_ref[:, 0:HALF] = left - dot_full(right, weights, 1, 1)
 
 
 def on_device(
@@ -405,17 +379,17 @@
             pltpu.VMEM((groups, height, R), jnp.float32),
             pltpu.VMEM((groups, 2, B, R), jnp.bfloat16),
             pltpu.VMEM((groups, 2, B, R), jnp.bfloat16),
-            pltpu.VMEM((groups, 8, R), jnp.int32),
-            pltpu.VMEM((groups, 8, R), jnp.int32),
+            pltpu.VMEM((groups, 8, HALF), jnp.int32),
+            pltpu.VMEM((groups, 8, HALF), jnp.int32),
             pltpu.SMEM((groups,), jnp.int32),
             pltpu.SMEM((groups,), jnp.int32),
             pltpu.VMEM((HALF, HALF), jnp.float32),
             pltpu.VMEM((HALF, HALF), jnp.float32),
             dma((7,)),
-            dma((2, members // 2, 3)),
+            dma,
             dma((2, members // 2, 3)),
         ]
-        + [dma((groups,))] * 8,
+        + [dma] * 8,
         compiler_params=pltpu.CompilerParams(
             collective_id=0, has_side_effects=True, vmem_limit_bytes=60 << 20
         ),

time: 66.4 us -> 61.5 us (0.926)
  Pallas kernels: 64.1 us -> 59.2 us
    pallas_call x1, Pallas kernels: 64.1 us -> 59.2 us  [on_device(): pl.pallas_call(functools.partial(update_kernel, groups, members), out_sha...]
where the time goes in v3:
time: 61.5 us; the launch traced here: 61.3 us
  Pallas kernels  59.2 us (96%)
  local copies, waits for them, and re-layouts  1.47 us (2%)
  between operations  0.66 us (1%)
    pallas_call x1, Pallas kernels, on_device(): pl.pallas_call(functools.partial(update_kernel, groups, members), out_sha...  59.2 us
    unnamed x1, local copies, waits for them, and re-layouts  1.47 us

profile of v3, /device:TPU:1, one launch (start us, length us, event | category | flops | bytes accessed | tf_op | source)
XLA Modules:
  0.0 61.3 jit_solution(13649089701279941817)
XLA Ops:
  0.7 59.2 %update_rows.1 = f32[64,256]{1,0:T(8,128)} custom-call(s32[4,8]{1,0:T(4,128)} %coords_hbm.1, s32[1,1]{1,0:T(1,128)S(6)} %copy.9.live_hbm, s32[1,128]{1,0:T(1,128)} %order_hbm.1, bf16[8,256,256]{2,1,0:T(8,128)(2,1)} %blocks_hbm.1, bf16[2,16,256]{2,1,0:T(8,128)(2,1)} %bitcast.5, bf16[2,16,256]{2,1,0:T(8,128)(2,1)} %bitcast.6, bf16[2,16,256]{2,1,0:T(8,128)(2,1)} %bitcast.7), custom_call_target="tpu_custom_call" | custom-call | tf_op jit(solution)/shard_map/update_rows/pallas_call | solution.py:365
  59.8 1.5 %copy.10 = f32[1,64,256]{2,1,0:T(8,128)} copy(f32[1,64,256]{2,1,0:T(8,128)} %bitcast.4) | data formatting | bytes 131072

commit v4 on v3

--- a/solution.py
+++ b/solution.py
@@ -210,7 +210,6 @@
         others = buffer.at[pl.ds(0, groups - 1)]
         pltpu.make_async_copy(others, others, sem).wait()
 
-    gram_set = (gram_out, gram_in, gram_send, gram_recv)
     rows_set = (rows_out, rows_in, rows_send, rows_recv)
     code_set = (code_out, code_in, code_send, code_recv)
 
@@ -242,6 +241,23 @@
 
     for distance in range(2, reach[0], 2):
         relay(distance)
+    gram_parts = {0: (0, 1), 2: (1, 2)}
+
+    def start_gram(start, count):
+        def one(step, carry):
+            target = lax.rem(group + step, groups)
+            pltpu.make_async_remote_copy(
+                src_ref=gram_out.at[target, pl.ds(start, count)],
+                dst_ref=gram_in.at[group, pl.ds(start, count)],
+                send_sem=gram_send,
+                recv_sem=gram_recv,
+                device_id={"grp": target},
+                device_id_type=MESH,
+            ).start()
+            return carry
+
+        lax.fori_loop(1, groups, one, 0, unroll=True)
+
     height = R // groups
     for mode in range(3):
         for distance in range(1, reach[0] + 1, 2):
@@ -255,7 +271,8 @@
             factor, factor, (((0,), (0,)), ((), ())), preferred_element_type=jnp.float32
         )
         gram_out[:, mode] = gram.reshape(groups, height, R)
-    start_all(gram_set)
+        if mode in gram_parts:
+            start_gram(*gram_parts[mode])
     load.wait()
 
     def one_slot(j, carry):

time: 61.5 us -> 60.8 us (0.989)
  Pallas kernels: 59.2 us -> 58.5 us
    pallas_call x1, Pallas kernels: 59.2 us -> 58.5 us  [on_device(): pl.pallas_call(functools.partial(update_kernel, groups, members), out_sha...]
where the time goes in v4:
time: 60.8 us; the launch traced here: 60.6 us
  Pallas kernels  58.5 us (96%)
  local copies, waits for them, and re-layouts  1.47 us (2%)
  between operations  0.66 us (1%)
    pallas_call x1, Pallas kernels, on_device(): pl.pallas_call(functools.partial(update_kernel, groups, members), out_sha...  58.5 us
    unnamed x1, local copies, waits for them, and re-layouts  1.47 us

profile of v4, /device:TPU:1, one launch (start us, length us, event | category | flops | bytes accessed | tf_op | source)
XLA Modules:
  0.0 60.6 jit_solution(13638805414673747870)
XLA Ops:
  0.7 58.5 %update_rows.1 = f32[64,256]{1,0:T(8,128)} custom-call(s32[4,8]{1,0:T(4,128)} %coords_hbm.1, s32[1,1]{1,0:T(1,128)S(6)} %copy.9.live_hbm, s32[1,128]{1,0:T(1,128)} %order_hbm.1, bf16[8,256,256]{2,1,0:T(8,128)(2,1)} %blocks_hbm.1, bf16[2,16,256]{2,1,0:T(8,128)(2,1)} %bitcast.5, bf16[2,16,256]{2,1,0:T(8,128)(2,1)} %bitcast.6, bf16[2,16,256]{2,1,0:T(8,128)(2,1)} %bitcast.7), custom_call_target="tpu_custom_call" | custom-call | tf_op jit(solution)/shard_map/update_rows/pallas_call | solution.py:382
  59.2 1.5 %copy.10 = f32[1,64,256]{2,1,0:T(8,128)} copy(f32[1,64,256]{2,1,0:T(8,128)} %bitcast.4) | data formatting | bytes 131072

commit v5 on v4

--- a/solution.py
+++ b/solution.py
@@ -241,7 +241,7 @@
 
     for distance in range(2, reach[0], 2):
         relay(distance)
-    gram_parts = {0: (0, 1), 2: (1, 2)}
+    gram_parts = {mode: (mode, 1) for mode in range(3)}
 
     def start_gram(start, count):
         def one(step, carry):

time: 60.8 us -> 61.2 us (level)
  no operation moved by 1% of the time
where the time goes in v5:
time: 61.2 us; the launch traced here: 61 us
  Pallas kernels  58.9 us (96%)
  local copies, waits for them, and re-layouts  1.47 us (2%)
  between operations  0.66 us (1%)
    pallas_call x1, Pallas kernels, on_device(): pl.pallas_call(functools.partial(update_kernel, groups, members), out_sha...  58.9 us
    unnamed x1, local copies, waits for them, and re-layouts  1.47 us

profile of v5, /device:TPU:1, one launch (start us, length us, event | category | flops | bytes accessed | tf_op | source)
XLA Modules:
  0.0 61.0 jit_solution(12291254728492748919)
XLA Ops:
  0.7 58.9 %update_rows.1 = f32[64,256]{1,0:T(8,128)} custom-call(s32[4,8]{1,0:T(4,128)} %coords_hbm.1, s32[1,1]{1,0:T(1,128)S(6)} %copy.9.live_hbm, s32[1,128]{1,0:T(1,128)} %order_hbm.1, bf16[8,256,256]{2,1,0:T(8,128)(2,1)} %blocks_hbm.1, bf16[2,16,256]{2,1,0:T(8,128)(2,1)} %bitcast.5, bf16[2,16,256]{2,1,0:T(8,128)(2,1)} %bitcast.6, bf16[2,16,256]{2,1,0:T(8,128)(2,1)} %bitcast.7), custom_call_target="tpu_custom_call" | custom-call | tf_op jit(solution)/shard_map/update_rows/pallas_call | solution.py:382
  59.6 1.5 %copy.10 = f32[1,64,256]{2,1,0:T(8,128)} copy(f32[1,64,256]{2,1,0:T(8,128)} %bitcast.4) | data formatting | bytes 131072
